TPU v7x, 512 devices: a whole 4x4x16 slice. The times are simulated.
512 devices in a mesh: seq: 64 (over z, y_lo, core), head: 8 (over y_hi, x).
Axes of the slice: x: 4, y: 4 (y_hi: 2, y_lo: 2; y = y_hi * 2 + y_lo), z: 16, core: 2. Of those that a mesh axis runs over, the one named last changes fastest.
Arguments:
- query_states: bfloat16 [8192, 3072], P(('seq', 'head')), may hold values from -48 to 48
- key_states: bfloat16 [8192, 3072], P(('seq', 'head')), may hold values from -9 to 9
- value_states: bfloat16 [8192, 3072], P(('seq', 'head')), may hold values from -6 to 6
- base_patch: bfloat16 [8192, 64], P(('seq', 'head')), may hold values from -4 to 4
- head_proj: bfloat16 [3072, 64], P('head'), may hold values from -0.4375 to 0.4375
- latent_std: float32 [16], replicated, may hold values from 0.5 to 2
- latent_mean: float32 [16], replicated, may hold values from -1 to 1
- w_in: bfloat16 [3, 3, 3, 16, 384], replicated, may hold values from -0.3125 to 0.3125
- b_in: float32 [384], replicated, may hold values from -0.5 to 0.5
- gain_mid: float32 [384], replicated, may hold values from 0.25 to 1.75
- w_up: bfloat16 [3, 3, 384, 192], replicated, may hold values from -0.109375 to 0.109375
- b_up: float32 [192], replicated, may hold values from -0.5 to 0.5
Outputs:
- video_features: bfloat16 [16, 256, 32, 192], P('head', 'seq')
All inputs are finite; a program needn't handle non-finite values.
Results may differ from a plain program's by a relative error of at most 0.017.
Values may be sent and summed in bfloat16 or wider, within the bound.
A program may use at most 64 MiB of HBM per device.

v0:
```python
import math

import jax
import jax.numpy as jnp
from jax import lax
from jax.experimental import pallas as pl
from jax.experimental.pallas import tpu as pltpu
from jax.sharding import PartitionSpec as P

MESH = pl.DeviceIdType.MESH
F32, BF16 = jnp.float32, jnp.bfloat16

SEQ, GROUPS = 64, 8
ROWS = 4
PLACES = ROWS * GROUPS
OWN = 16
ROW = OWN * GROUPS
PLANE = ROW * ROWS
HD, LOCAL = 128, 3
WIDE = HD * LOCAL
PATCH = 64
NUM = PATCH * LOCAL
MSG = 256
TALL = PATCH + 8
CH, OUTCH = 384, 192
EDGE = 8
LINE = 48
TO_LOG2 = math.log2(math.e) / math.sqrt(HD)


def dot(a, b, dims):
    return lax.dot_general(a, b, (dims, ((), ())), preferred_element_type=F32)


def kernel(
    q_in, k_in, v_in, base_far, proj_far, std_far, mean_far, w_in_far, b_in_far, gain_far, w_up_far, b_up_far,
    out_ref,
    keys, values, v_row, queries, turned_queries, top, fade, weighted, summed, turned, sending, parts, lat_own, lat_near,
    base_ref, proj_ref, std_ref, mean_ref, w_in, b_in_ref, gain_ref, w_up, b_up_ref, w_two, enlarged, columns,
    plane_send, plane_recv, ring_send, ring_recv, part_send, part_recv, near_send, near_recv, weight_sem,
):
    s, g = lax.axis_index("seq"), lax.axis_index("head")
    z, row = s // ROWS, s % ROWS
    place = row * GROUPS + g
    up, down = ((s + ROWS) % SEQ, g), ((s + SEQ - ROWS) % SEQ, g)
    after, before = (s + 1) % SEQ, (s + SEQ - 1) % SEQ
    next_g, last_g = (g + 1) % GROUPS, (g + GROUPS - 1) % GROUPS

    def peer(i):
        other = (place + i) % PLACES
        return other, (z * ROWS + other // GROUPS, other % GROUPS)

    def columns_of(group):
        return pl.ds(pl.multiple_of(group * WIDE, WIDE), WIDE)

    def tokens_of(index):
        return pl.ds(pl.multiple_of(index * OWN, OWN), OWN)

    barrier = pltpu.get_barrier_semaphore()

    for i in range(1, PLACES):
        pl.semaphore_signal(barrier, inc=1, device_id=peer(i)[1], device_id_type=MESH)
    for other in (up, down, (after, g), (before, g), (after, last_g), (before, last_g)):
        pl.semaphore_signal(barrier, inc=1, device_id=other, device_id_type=MESH)

    rows_of = ((k_in, keys.at[0]), (v_in, v_row))
    for kind, (source, target) in enumerate(rows_of):
        pltpu.make_async_copy(source.at[:, columns_of(g)], target.at[tokens_of(g)], plane_recv.at[kind]).start()
    pltpu.make_async_copy(q_in.at[:, columns_of(g)], queries.at[tokens_of(place)], plane_recv.at[2]).start()
    proj_in = pltpu.make_async_copy(proj_far, proj_ref, weight_sem.at[8])
    proj_in.start()
    pl.semaphore_wait(barrier, PLACES - 1 + 6)

    for kind, (source, target) in enumerate(rows_of):
        for i in range(1, GROUPS):
            other = (g + i) % GROUPS
            pltpu.make_async_remote_copy(
                src_ref=source.at[:, columns_of(other)],
                dst_ref=target.at[tokens_of(g)],
                send_sem=plane_send.at[kind],
                recv_sem=plane_recv.at[kind],
                device_id=(s, other),
                device_id_type=MESH,
            ).start()

    def portion(kind, slot, part):
        return values.at[slot] if kind else keys.at[slot, pl.ds(part * ROW // 2, ROW // 2)]

    def hop(kind, source, target, way, part):
        pltpu.make_async_remote_copy(
            src_ref=portion(kind, source, part),
            dst_ref=portion(kind, target, part),
            send_sem=ring_send.at[way, kind],
            recv_sem=ring_recv.at[kind, target, part],
            device_id=(up, down)[way],
            device_id_type=MESH,
        ).start()

    def arrived(kind, slot, part):
        pltpu.make_async_copy(
            portion(kind, slot, part), portion(kind, slot, part), ring_recv.at[kind, slot, part]
        ).wait()

    for kind, (source, target) in enumerate(rows_of):
        pltpu.make_async_copy(target, target, plane_recv.at[kind]).wait()
        if kind == 1:
            proj_in.wait()
            for h in range(LOCAL):
                lanes = slice(h * HD, h * HD + HD)
                values[0, h * PATCH : h * PATCH + PATCH, :] = dot(
                    proj_ref[:, lanes], v_row[:, lanes], ((1,), (1,))
                ).astype(BF16)
        for part in range(2 - kind):
            hop(kind, 0, 1, 0, part)
            hop(kind, 0, 9, 1, part)

    for i in range(1, PLACES):
        device = peer(i)[1]
        pltpu.make_async_remote_copy(
            src_ref=q_in.at[:, columns_of(device[1])],
            dst_ref=queries.at[tokens_of(place)],
            send_sem=plane_send.at[2],
            recv_sem=plane_recv.at[2],
            device_id=device,
            device_id_type=MESH,
        ).start()

    parameters = [
        pltpu.make_async_copy(source, target, weight_sem.at[i])
        for i, (source, target) in enumerate(
            (
                (w_in_far, w_in),
                (w_up_far, w_up),
                (base_far, base_ref),
                (std_far, std_ref),
                (mean_far, mean_ref),
                (b_in_far, b_in_ref),
                (gain_far, gain_ref),
                (b_up_far, b_up_ref),
            )
        )
    ]
    for copy in parameters:
        copy.start()

    for copy in parameters:
        copy.wait()
    w_two[...] = jnp.zeros_like(w_two)
    for t in range(3):
        for u in range(3):
            piece = w_in[(t * 3 + u) * 48 : (t * 3 + u) * 48 + 48, :]
            for half in range(2):
                at = t * 256 + (u + half) * 64
                w_two[at : at + 48, half * CH : half * CH + CH] = piece
    enlarged[...] = jnp.zeros_like(enlarged)
    turned[...] = jnp.zeros_like(turned)

    def joined(pieces, axis):
        return pieces[0] if len(pieces) == 1 else jnp.concatenate(pieces, axis=axis)

    units = [
        (h, slice(h * HD, h * HD + HD), slice(c * 256, c * 256 + 256)) for h in range(LOCAL) for c in range(2)
    ]

    def add_up(slots, chosen, first=False):
        for h, lanes, some in chosen:
            some_values = joined([values[slot, h * PATCH : h * PATCH + PATCH, :] for slot in slots], 1)
            some_values = jnp.concatenate([some_values, jnp.ones((16, len(slots) * ROW), BF16)], axis=0)
            product = dot(some_values, weighted[h, : len(slots) * ROW, some], ((1,), (0,)))[:TALL]
            rows = slice(h * TALL, h * TALL + TALL)
            summed[rows, some] = product if first else summed[rows, some] * fade[h : h + 1, some] + product

    def attend(earlier, slots, chosen):
        scores = [
            dot(joined([keys[slot, :, lanes] for slot in slots], 0), turned_queries[lanes, some], ((1,), (0,)))
            for h, lanes, some in chosen
        ]
        if earlier:
            add_up(earlier, chosen, first=earlier == [0])
        for (h, lanes, some), score in zip(chosen, scores):
            new = jnp.max(score, axis=0, keepdims=True)
            if earlier:
                old = top[h : h + 1, some]
                new = jnp.maximum(old, new)
                fading = jnp.exp2((old - new) * TO_LOG2)
                fade[h : h + 1, some] = fading
            weights = jnp.exp2((score - new) * TO_LOG2)
            top[h : h + 1, some] = new
            weighted[h, : len(slots) * ROW, some] = weights.astype(BF16)

    some, rest = units[:3], units[3:]

    def pass_on(kind, t, part):
        arrived(kind, t, part)
        hop(kind, t, t + 1, 0, part)
        arrived(kind, t + 8, part)
        hop(kind, t + 8, t + 9, 1, part)

    pass_on(0, 1, 0)
    pass_on(0, 1, 1)
    pass_on(1, 1, 0)
    pltpu.make_async_copy(queries, queries, plane_recv.at[2]).wait()
    turned_queries[...] = queries[...].T
    attend([], [0], units)
    pass_on(0, 2, 0)
    pass_on(0, 2, 1)
    attend([0], [1, 9], some)
    pass_on(1, 2, 0)
    attend([0], [1, 9], rest)

    def step(t, carry):
        for event, (kind, part) in enumerate(((0, 0), (0, 1), (1, 0))):
            pass_on(kind, t, part)
            attend([t - 2, t + 6], [t - 1, t + 7], units[event * 2 : event * 2 + 2])
        return carry

    lax.fori_loop(3, 7, step, 0)
    for part in range(2):
        arrived(0, 7, part)
        hop(0, 7, 8, 0, part)
        arrived(0, 15, part)
        attend([5, 13], [6, 14], units[part * 2 : part * 2 + 2])
    arrived(1, 15, 0)
    hop(1, 15, 8, 1, 0)
    arrived(1, 7, 0)
    attend([5, 13], [6, 14], units[4:])
    attend([6, 14], [7, 15], units)
    for part in range(2):
        arrived(0, 8, part)
    attend([7, 15], [8], units)
    arrived(1, 8, 0)
    add_up([8], units)

    for h in range(LOCAL):
        sums = summed[h * TALL + PATCH : h * TALL + PATCH + 1, :]
        turned[h * PATCH : h * PATCH + PATCH, :] = summed[h * TALL : h * TALL + PATCH, :] * (1.0 / sums)
        level = top[h : h + 1, :] * TO_LOG2 + jnp.log(sums) * math.log2(math.e)
        for term in range(3):
            rounded = level.astype(BF16).astype(F32)
            turned[NUM + term * LOCAL + h : NUM + term * LOCAL + h + 1, :] = rounded
            level = level - rounded
    for away in (1, 2, 3, 0):
        to_row = (row + away) % ROWS
        lanes = pl.ds(pl.multiple_of(to_row * ROW, ROW), ROW)
        sending[lanes, :] = turned[:, lanes].astype(BF16).T
        if away == 0:
            pltpu.make_async_copy(sending.at[tokens_of(place)], parts.at[tokens_of(place)], part_recv).start()
        for i in range(0 if away else 1, GROUPS):
            to_group = (g + i) % GROUPS
            pltpu.make_async_remote_copy(
                src_ref=sending.at[tokens_of(to_row * GROUPS + to_group)],
                dst_ref=parts.at[tokens_of(place)],
                send_sem=part_send,
                recv_sem=part_recv,
                device_id=(z * ROWS + to_row, to_group),
                device_id_type=MESH,
            ).start()

    def ones_where(shape, made):
        r = lax.broadcasted_iota(jnp.int32, shape, 0)
        c = lax.broadcasted_iota(jnp.int32, shape, 1)
        return made(r, c).astype(F32).astype(BF16)

    spread = ones_where(
        (MSG, NUM),
        lambda r, c: (r >= NUM) & (r < NUM + 3 * LOCAL) & ((r - NUM) % LOCAL == c // PATCH),
    )
    pltpu.make_async_copy(parts, parts, part_recv).wait()

    levels = dot(parts[...], spread, ((1,), (0,)))
    numbers = parts[:, :NUM].astype(F32)
    by_row = [slice(r * ROW, r * ROW + ROW) for r in range(ROWS)]
    highest = levels[by_row[0]]
    for r in range(1, ROWS):
        highest = jnp.maximum(highest, levels[by_row[r]])
    above, below = 0.0, 0.0
    for r in range(ROWS):
        share = jnp.exp2(levels[by_row[r]] - highest)
        above = above + share * numbers[by_row[r]]
        below = below + share
    merged = above / below
    tokens = merged[:OWN]
    for other in range(1, GROUPS):
        tokens = tokens + merged[other * OWN : other * OWN + OWN]
    patch = base_ref[...].astype(F32)
    for h in range(LOCAL):
        patch = patch + tokens[:, h * PATCH : h * PATCH + PATCH]
    std = jnp.concatenate([std_ref[...]] * 4, axis=1)
    mean = jnp.concatenate([mean_ref[...]] * 4, axis=1)
    latent = patch * std + mean
    lat_own[...] = jnp.concatenate([latent, latent], axis=1).astype(BF16)

    for slot, device in enumerate(((after, next_g), (after, g), (s, next_g), (before, next_g), (before, g))):
        pltpu.make_async_remote_copy(
            src_ref=lat_own,
            dst_ref=lat_near.at[slot],
            send_sem=near_send,
            recv_sem=near_recv,
            device_id=device,
            device_id_type=MESH,
        ).start()

    def picks(b):
        def made(r, c):
            a, v, low = c // 64, (c // 16) % 4, c % 16
            spot = v + 1 - b
            wanted = (spot // 2) * 64 + a * 32 + (spot % 2) * 16 + low
            return (v < 3) & (r == wanted)

        return ones_where((128, 128), made)

    pick = [picks(0), picks(1)]
    pltpu.make_async_copy(lat_near, lat_near, near_recv).wait()

    has_before = (s > 0).astype(F32)
    has_after = (s < SEQ - 1).astype(F32)
    has_frames = (g > 0).astype(F32)
    tiles = [
        [lat_near[0].astype(F32) * (has_before * has_frames), lat_near[1].astype(F32) * has_before],
        [lat_near[2].astype(F32) * has_frames, lat_own[...].astype(F32)],
        [lat_near[3].astype(F32) * (has_after * has_frames), lat_near[4].astype(F32) * has_after],
    ]
    lane = lax.broadcasted_iota(jnp.int32, (8, 128), 1)
    line = lax.broadcasted_iota(jnp.int32, (8, 128), 0)
    sides = ([], [])
    for f in range(4):
        for r in range(3):
            here = tiles[r][f // 2][(f % 2) * 8 : (f % 2) * 8 + 8]
            left = jnp.where(line == 0, 0.0, pltpu.roll(here, 1, 0))
            right = jnp.where(line == 7, 0.0, pltpu.roll(here, 7, 0))
            sides[0].append(jnp.where(lane < 64, left, here))
            sides[1].append(jnp.where(lane < 64, here, right))
    windows = [
        dot(jnp.concatenate(side, axis=0).astype(BF16), chosen, ((1,), (0,))) for side, chosen in zip(sides, pick)
    ]

    def window(f, r, b):
        at = (f * 3 + r) * 8
        return windows[b][at : at + 8]

    lines = []
    for f in range(2):
        for pair in range(2):
            for b in range(2):
                pieces = [window(f + t, pair + r, b) for t in range(3) for r in range(2)]
                lines.append(jnp.concatenate(pieces, axis=1))
    conv = dot(jnp.concatenate(lines, axis=0).astype(BF16), w_two[...], ((1,), (0,)))
    for half in range(2):
        out = conv[:, half * CH : half * CH + CH] + b_in_ref[...].reshape(1, CH)
        mean_sq = jnp.mean(out * out, axis=1, keepdims=True)
        normed = out * lax.rsqrt(mean_sq + 1e-6) * gain_ref[...].reshape(1, CH)
        active = normed / (1.0 + jnp.exp(-normed))
        for f in range(2):
            for pair in range(2):
                y = 2 * pair + half
                for b in range(2):
                    at = ((f * 2 + pair) * 2 + b) * 8
                    part = active[at : at + 8]
                    if y == 0:
                        part = part * has_before
                    if y == 3:
                        part = part * has_after
                    for twice in range(2):
                        for tile in range(3):
                            enlarged[tile, f * 4 + y, pl.ds(EDGE + 2 * b + twice, 8, stride=4), :] = part[
                                :, tile * 128 : tile * 128 + 128
                            ]

    for v in range(3):
        for f in range(2):
            for y in range(4):
                piece = [enlarged[tile, f * 4 + y, EDGE - 1 + v : EDGE + 31 + v, :] for tile in range(3)]
                piece = jnp.concatenate(piece, axis=1).astype(BF16)
                for line_out in range(4):
                    for u in range(3):
                        if (line_out + u + 1) // 2 == y:
                            at = (f * 4 + line_out) * 32
                            to = (u * 3 + v) * CH
                            columns[at : at + 32, to : to + CH] = piece
    planes = b_up_ref[...]
    for tap in range(9):
        planes = planes + dot(
            columns[:, tap * CH : tap * CH + CH], w_up[tap * OUTCH : tap * OUTCH + OUTCH, :], ((1,), (1,))
        )
    out_ref[...] = planes.astype(BF16)

    for kind in (0, 1):
        sent = v_row.at[: ROW - OWN]
        pltpu.make_async_copy(sent, sent, plane_send.at[kind]).wait()
    sent = queries.at[: PLANE - OWN]
    pltpu.make_async_copy(sent, sent, plane_send.at[2]).wait()
    for way, kind, ring, count in ((0, 0, keys, 8), (0, 1, values, 7), (1, 0, keys, 7), (1, 1, values, 8)):
        sent = ring.at[:count]
        pltpu.make_async_copy(sent, sent, ring_send.at[way, kind]).wait()
    sent = parts.at[: PLANE - OWN]
    pltpu.make_async_copy(sent, sent, part_send).wait()
    pltpu.make_async_copy(lat_near, lat_near, near_send).wait()


def on_device(
    query_states,
    key_states,
    value_states,
    base_patch,
    head_proj,
    latent_std,
    latent_mean,
    w_in,
    b_in,
    gain_mid,
    w_up,
    b_up,
):
    here = pl.BlockSpec(memory_space=pltpu.VMEM)
    far = pl.BlockSpec(memory_space=pltpu.HBM)
    DMA = pltpu.SemaphoreType.DMA
    planes = pl.pallas_call(
        kernel,
        out_shape=pltpu.VMEM((256, OUTCH), BF16),
        in_specs=[far] * 12,
        out_specs=here,
        scratch_shapes=[
            pltpu.VMEM((16, ROW, WIDE), BF16),
            pltpu.VMEM((16, NUM, ROW), BF16),
            pltpu.VMEM((ROW, WIDE), BF16),
            pltpu.VMEM((PLANE, WIDE), BF16),
            pltpu.VMEM((WIDE, PLANE), BF16),
            pltpu.VMEM((8, PLANE), F32),
            pltpu.VMEM((8, PLANE), F32),
            pltpu.VMEM((LOCAL, 2 * ROW, PLANE), BF16),
            pltpu.VMEM((LOCAL * TALL, PLANE), F32),
            pltpu.VMEM((MSG, PLANE), F32),
            pltpu.VMEM((PLANE, MSG), BF16),
            pltpu.VMEM((PLANE, MSG), BF16),
            pltpu.VMEM((OWN, 128), BF16),
            pltpu.VMEM((5, OWN, 128), BF16),
            pltpu.VMEM((OWN, PATCH), BF16),
            pltpu.VMEM((PATCH, WIDE), BF16),
            pltpu.VMEM((1, 16), F32),
            pltpu.VMEM((1, 16), F32),
            pltpu.VMEM((27 * 16, CH), BF16),
            pltpu.VMEM((CH,), F32),
            pltpu.VMEM((CH,), F32),
            pltpu.VMEM((9 * OUTCH, CH), BF16),
            pltpu.VMEM((1, OUTCH), F32),
            pltpu.VMEM((768, 2 * CH), BF16),
            pltpu.VMEM((3, 8, LINE, 128), F32),
            pltpu.VMEM((256, 9 * CH), BF16),
            DMA((3,)),
            DMA((3,)),
            DMA((2, 2)),
            DMA((2, 16, 2)),
            DMA,
            DMA,
            DMA,
            DMA,
            DMA((9,)),
        ],
        compiler_params=pltpu.CompilerParams(
            collective_id=0, has_side_effects=True, vmem_limit_bytes=60 * 1024 * 1024
        ),
        name="attend_and_decode",
    )(
        query_states,
        key_states,
        value_states,
        base_patch,
        head_proj.T,
        latent_std.reshape(1, 16),
        latent_mean.reshape(1, 16),
        w_in.reshape(27 * 16, CH),
        b_in,
        gain_mid,
        w_up.transpose(0, 1, 3, 2).reshape(9 * OUTCH, CH),
        b_up.reshape(1, OUTCH),
    )
    return planes.reshape(2, 4, 32, OUTCH)


def solution(mesh):
    in_specs = (
        P(("seq", "head"), None),
        P(("seq", "head"), None),
        P(("seq", "head"), None),
        P(("seq", "head"), None),
        P("head", None),
        P(),
        P(),
        P(),
        P(),
        P(),
        P(),
        P(),
    )
    out_specs = P("head", "seq", None, None)
    return jax.shard_map(
        on_device, mesh=mesh, in_specs=in_specs, out_specs=out_specs, check_vma=False
    )
```

profile of v0, /device:TPU:1, one launch (start us, length us, event | category | flops | bytes accessed | tf_op | source)
XLA Modules:
  0.0 66.6 jit_solution(4346776771861353299)
XLA Ops:
  0.0 66.0 %attend_and_decode.1 = bf16[256,192]{1,0:T(8,128)(2,1)S(1)} custom-call(bf16[16,3072]{1,0:T(8,128)(2,1)} %q_in.1, bf16[16,3072]{1,0:T(8,128)(2,1)} %k_in.1, bf16[16,3072]{1,0:T(8,128)(2,1)} %v_in.1, bf16[16,64]{1,0:T(8,128)(2,1)} %base_far.1, bf16[64,384]{1,0:T(8,128)(2,1)} %bitcast.12, f32[1,16]{1,0:T(1,128)} %bitcast.14, f32[1,16]{1,0:T(1,128)} %bitcast.15, ...), custom_call_target="tpu_custom_call" | custom-call | tf_op jit(solution)/shard_map/attend_and_decode/pallas_call | solution.py:417
  66.0 0.7 copy.14
where the time goes:
time: 66.8 us; the launch traced here: 66.6 us
  Pallas kernels  66 us (99%)
    pallas_call x1, Pallas kernels, on_device(): pl.pallas_call(kernel, out_shape=pltpu.VMEM((256, OUTCH), BF16), in_specs...  66 us

commit v1 on v0

--- a/solution.py
+++ b/solution.py
@@ -63,10 +63,10 @@
     for other in (up, down, (after, g), (before, g), (after, last_g), (before, last_g)):
         pl.semaphore_signal(barrier, inc=1, device_id=other, device_id_type=MESH)
 
-    rows_of = ((k_in, keys.at[0]), (v_in, v_row))
+    q_row = queries.at[pl.ds(pl.multiple_of(row * ROW, ROW), ROW)]
+    rows_of = ((k_in, keys.at[0]), (v_in, v_row), (q_in, q_row))
     for kind, (source, target) in enumerate(rows_of):
         pltpu.make_async_copy(source.at[:, columns_of(g)], target.at[tokens_of(g)], plane_recv.at[kind]).start()
-    pltpu.make_async_copy(q_in.at[:, columns_of(g)], queries.at[tokens_of(place)], plane_recv.at[2]).start()
     proj_in = pltpu.make_async_copy(proj_far, proj_ref, weight_sem.at[8])
     proj_in.start()
     pl.semaphore_wait(barrier, PLACES - 1 + 6)
@@ -101,7 +101,7 @@
             portion(kind, slot, part), portion(kind, slot, part), ring_recv.at[kind, slot, part]
         ).wait()
 
-    for kind, (source, target) in enumerate(rows_of):
+    for kind, (source, target) in enumerate(rows_of[:2]):
         pltpu.make_async_copy(target, target, plane_recv.at[kind]).wait()
         if kind == 1:
             proj_in.wait()
@@ -114,14 +114,14 @@
             hop(kind, 0, 1, 0, part)
             hop(kind, 0, 9, 1, part)
 
-    for i in range(1, PLACES):
-        device = peer(i)[1]
+    pltpu.make_async_copy(q_row, q_row, plane_recv.at[2]).wait()
+    for i in range(1, ROWS):
         pltpu.make_async_remote_copy(
-            src_ref=q_in.at[:, columns_of(device[1])],
-            dst_ref=queries.at[tokens_of(place)],
-            send_sem=plane_send.at[2],
-            recv_sem=plane_recv.at[2],
-            device_id=device,
+            src_ref=q_row,
+            dst_ref=q_row,
+            send_sem=plane_send.at[3],
+            recv_sem=plane_recv.at[3],
+            device_id=(z * ROWS + (row + i) % ROWS, g),
             device_id_type=MESH,
         ).start()
 
@@ -175,11 +175,12 @@
             dot(joined([keys[slot, :, lanes] for slot in slots], 0), turned_queries[lanes, some], ((1,), (0,)))
             for h, lanes, some in chosen
         ]
+        first = earlier == []
         if earlier:
             add_up(earlier, chosen, first=earlier == [0])
         for (h, lanes, some), score in zip(chosen, scores):
             new = jnp.max(score, axis=0, keepdims=True)
-            if earlier:
+            if not first:
                 old = top[h : h + 1, some]
                 new = jnp.maximum(old, new)
                 fading = jnp.exp2((old - new) * TO_LOG2)
@@ -199,7 +200,8 @@
     pass_on(0, 1, 0)
     pass_on(0, 1, 1)
     pass_on(1, 1, 0)
-    pltpu.make_async_copy(queries, queries, plane_recv.at[2]).wait()
+    others = queries.at[: PLANE - ROW]
+    pltpu.make_async_copy(others, others, plane_recv.at[3]).wait()
     turned_queries[...] = queries[...].T
     attend([], [0], units)
     pass_on(0, 2, 0)
@@ -225,9 +227,10 @@
     arrived(1, 7, 0)
     attend([5, 13], [6, 14], units[4:])
     attend([6, 14], [7, 15], units)
+    add_up([7, 15], units)
     for part in range(2):
         arrived(0, 8, part)
-    attend([7, 15], [8], units)
+    attend(None, [8], units)
     arrived(1, 8, 0)
     add_up([8], units)
 
@@ -384,11 +387,11 @@
         )
     out_ref[...] = planes.astype(BF16)
 
-    for kind in (0, 1):
+    for kind in range(3):
         sent = v_row.at[: ROW - OWN]
         pltpu.make_async_copy(sent, sent, plane_send.at[kind]).wait()
-    sent = queries.at[: PLANE - OWN]
-    pltpu.make_async_copy(sent, sent, plane_send.at[2]).wait()
+    sent = queries.at[: PLANE - ROW]
+    pltpu.make_async_copy(sent, sent, plane_send.at[3]).wait()
     for way, kind, ring, count in ((0, 0, keys, 8), (0, 1, values, 7), (1, 0, keys, 7), (1, 1, values, 8)):
         sent = ring.at[:count]
         pltpu.make_async_copy(sent, sent, ring_send.at[way, kind]).wait()
@@ -446,8 +449,8 @@
             pltpu.VMEM((768, 2 * CH), BF16),
             pltpu.VMEM((3, 8, LINE, 128), F32),
             pltpu.VMEM((256, 9 * CH), BF16),
-            DMA((3,)),
-            DMA((3,)),
+            DMA((4,)),
+            DMA((4,)),
             DMA((2, 2)),
             DMA((2, 16, 2)),
             DMA,

time: 66.8 us -> 65.4 us (0.979)
  Pallas kernels: 66 us -> 64.5 us
    pallas_call x1, Pallas kernels: 66 us -> 64.5 us  [on_device(): pl.pallas_call(kernel, out_shape=pltpu.VMEM((256, OUTCH), BF16), in_specs...]
where the time goes in v1:
time: 65.4 us; the launch traced here: 65.2 us
  Pallas kernels  64.5 us (99%)
  local copies, waits for them, and re-layouts  0.66 us (1%)
    pallas_call x1, Pallas kernels, on_device(): pl.pallas_call(kernel, out_shape=pltpu.VMEM((256, OUTCH), BF16), in_specs...  64.5 us

profile of v1, /device:TPU:1, one launch (start us, length us, event | category | flops | bytes accessed | tf_op | source)
XLA Modules:
  0.0 65.2 jit_solution(11505327109581694587)
XLA Ops:
  0.0 64.5 %attend_and_decode.1 = bf16[256,192]{1,0:T(8,128)(2,1)S(1)} custom-call(bf16[16,3072]{1,0:T(8,128)(2,1)} %q_in.1, bf16[16,3072]{1,0:T(8,128)(2,1)} %k_in.1, bf16[16,3072]{1,0:T(8,128)(2,1)} %v_in.1, bf16[16,64]{1,0:T(8,128)(2,1)} %base_far.1, bf16[64,384]{1,0:T(8,128)(2,1)} %bitcast.12, f32[1,16]{1,0:T(1,128)} %bitcast.14, f32[1,16]{1,0:T(1,128)} %bitcast.15, ...), custom_call_target="tpu_custom_call" | custom-call | tf_op jit(solution)/shard_map/attend_and_decode/pallas_call | solution.py:420
  64.6 0.7 %copy.14 = bf16[2,4,32,192]{3,2,1,0:T(8,128)(2,1)} copy(bf16[2,4,32,192]{3,2,1,0:T(8,128)(2,1)S(1)} %bitcast.9) | data formatting | bytes 196608

commit v2 on v1

--- a/solution.py
+++ b/solution.py
@@ -36,7 +36,7 @@
     q_in, k_in, v_in, base_far, proj_far, std_far, mean_far, w_in_far, b_in_far, gain_far, w_up_far, b_up_far,
     out_ref,
     keys, values, v_row, queries, turned_queries, top, fade, weighted, summed, turned, sending, parts, lat_own, lat_near,
-    base_ref, proj_ref, std_ref, mean_ref, w_in, b_in_ref, gain_ref, w_up, b_up_ref, w_two, enlarged, columns,
+    base_ref, proj_ref, std_ref, mean_ref, w_in, b_in_ref, gain_ref, w_up, b_up_ref, w_two, enlarged, columns, spread, pick, affine,
     plane_send, plane_recv, ring_send, ring_recv, part_send, part_recv, near_send, near_recv, weight_sem,
 ):
     s, g = lax.axis_index("seq"), lax.axis_index("head")
@@ -65,8 +65,6 @@
 
     q_row = queries.at[pl.ds(pl.multiple_of(row * ROW, ROW), ROW)]
     rows_of = ((k_in, keys.at[0]), (v_in, v_row), (q_in, q_row))
-    for kind, (source, target) in enumerate(rows_of):
-        pltpu.make_async_copy(source.at[:, columns_of(g)], target.at[tokens_of(g)], plane_recv.at[kind]).start()
     proj_in = pltpu.make_async_copy(proj_far, proj_ref, weight_sem.at[8])
     proj_in.start()
     pl.semaphore_wait(barrier, PLACES - 1 + 6)
@@ -82,6 +80,7 @@
                 device_id=(s, other),
                 device_id_type=MESH,
             ).start()
+        pltpu.make_async_copy(source.at[:, columns_of(g)], target.at[tokens_of(g)], plane_recv.at[kind]).start()
 
     def portion(kind, slot, part):
         return values.at[slot] if kind else keys.at[slot, pl.ds(part * ROW // 2, ROW // 2)]
@@ -152,6 +151,7 @@
             for half in range(2):
                 at = t * 256 + (u + half) * 64
                 w_two[at : at + 48, half * CH : half * CH + CH] = piece
+
     enlarged[...] = jnp.zeros_like(enlarged)
     turned[...] = jnp.zeros_like(turned)
 
@@ -200,6 +200,30 @@
     pass_on(0, 1, 0)
     pass_on(0, 1, 1)
     pass_on(1, 1, 0)
+
+    def ones_where(shape, made):
+        r = lax.broadcasted_iota(jnp.int32, shape, 0)
+        c = lax.broadcasted_iota(jnp.int32, shape, 1)
+        return made(r, c).astype(F32).astype(BF16)
+
+    spread[...] = ones_where(
+        (MSG, NUM),
+        lambda r, c: (r >= NUM) & (r < NUM + 3 * LOCAL) & ((r - NUM) % LOCAL == c // PATCH),
+    )
+    def picks(b):
+        def made(r, c):
+            a, v, low = c // 64, (c // 16) % 4, c % 16
+            spot = v + 1 - b
+            wanted = (spot // 2) * 64 + a * 32 + (spot % 2) * 16 + low
+            return (v < 3) & (r == wanted)
+
+        return ones_where((128, 128), made)
+
+    pick[0] = picks(0)
+    pick[1] = picks(1)
+    for i, ref in enumerate((std_ref, mean_ref)):
+        affine[i : i + 1, :PATCH] = jnp.concatenate([ref[...]] * 4, axis=1)
+
     others = queries.at[: PLANE - ROW]
     pltpu.make_async_copy(others, others, plane_recv.at[3]).wait()
     turned_queries[...] = queries[...].T
@@ -259,18 +283,9 @@
                 device_id_type=MESH,
             ).start()
 
-    def ones_where(shape, made):
-        r = lax.broadcasted_iota(jnp.int32, shape, 0)
-        c = lax.broadcasted_iota(jnp.int32, shape, 1)
-        return made(r, c).astype(F32).astype(BF16)
-
-    spread = ones_where(
-        (MSG, NUM),
-        lambda r, c: (r >= NUM) & (r < NUM + 3 * LOCAL) & ((r - NUM) % LOCAL == c // PATCH),
-    )
     pltpu.make_async_copy(parts, parts, part_recv).wait()
 
-    levels = dot(parts[...], spread, ((1,), (0,)))
+    levels = dot(parts[...], spread[...], ((1,), (0,)))
     numbers = parts[:, :NUM].astype(F32)
     by_row = [slice(r * ROW, r * ROW + ROW) for r in range(ROWS)]
     highest = levels[by_row[0]]
@@ -288,9 +303,7 @@
     patch = base_ref[...].astype(F32)
     for h in range(LOCAL):
         patch = patch + tokens[:, h * PATCH : h * PATCH + PATCH]
-    std = jnp.concatenate([std_ref[...]] * 4, axis=1)
-    mean = jnp.concatenate([mean_ref[...]] * 4, axis=1)
-    latent = patch * std + mean
+    latent = patch * affine[0:1, :PATCH] + affine[1:2, :PATCH]
     lat_own[...] = jnp.concatenate([latent, latent], axis=1).astype(BF16)
 
     for slot, device in enumerate(((after, next_g), (after, g), (s, next_g), (before, next_g), (before, g))):
@@ -303,16 +316,6 @@
             device_id_type=MESH,
         ).start()
 
-    def picks(b):
-        def made(r, c):
-            a, v, low = c // 64, (c // 16) % 4, c % 16
-            spot = v + 1 - b
-            wanted = (spot // 2) * 64 + a * 32 + (spot % 2) * 16 + low
-            return (v < 3) & (r == wanted)
-
-        return ones_where((128, 128), made)
-
-    pick = [picks(0), picks(1)]
     pltpu.make_async_copy(lat_near, lat_near, near_recv).wait()
 
     has_before = (s > 0).astype(F32)
@@ -334,7 +337,7 @@
             sides[0].append(jnp.where(lane < 64, left, here))
             sides[1].append(jnp.where(lane < 64, here, right))
     windows = [
-        dot(jnp.concatenate(side, axis=0).astype(BF16), chosen, ((1,), (0,))) for side, chosen in zip(sides, pick)
+        dot(jnp.concatenate(side, axis=0).astype(BF16), chosen, ((1,), (0,))) for side, chosen in zip(sides, (pick[0], pick[1]))
     ]
 
     def window(f, r, b):
@@ -449,6 +452,9 @@
             pltpu.VMEM((768, 2 * CH), BF16),
             pltpu.VMEM((3, 8, LINE, 128), F32),
             pltpu.VMEM((256, 9 * CH), BF16),
+            pltpu.VMEM((MSG, NUM), BF16),
+            pltpu.VMEM((2, 128, 128), BF16),
+            pltpu.VMEM((8, 128), F32),
             DMA((4,)),
             DMA((4,)),
             DMA((2, 2)),

time: 65.4 us -> 65.4 us (level)
  no operation moved by 1% of the time
where the time goes in v2:
time: 65.4 us; the launch traced here: 65.2 us
  Pallas kernels  64.6 us (99%)
  local copies, waits for them, and re-layouts  0.66 us (1%)
    pallas_call x1, Pallas kernels, on_device(): pl.pallas_call(kernel, out_shape=pltpu.VMEM((256, OUTCH), BF16), in_specs...  64.6 us

profile of v2, /device:TPU:1, one launch (start us, length us, event | category | flops | bytes accessed | tf_op | source)
XLA Modules:
  0.0 65.2 jit_solution(14712937411490166601)
XLA Ops:
  0.0 64.6 %attend_and_decode.1 = bf16[256,192]{1,0:T(8,128)(2,1)S(1)} custom-call(bf16[16,3072]{1,0:T(8,128)(2,1)} %q_in.1, bf16[16,3072]{1,0:T(8,128)(2,1)} %k_in.1, bf16[16,3072]{1,0:T(8,128)(2,1)} %v_in.1, bf16[16,64]{1,0:T(8,128)(2,1)} %base_far.1, bf16[64,384]{1,0:T(8,128)(2,1)} %bitcast.12, f32[1,16]{1,0:T(1,128)} %bitcast.14, f32[1,16]{1,0:T(1,128)} %bitcast.15, ...), custom_call_target="tpu_custom_call" | custom-call | tf_op jit(solution)/shard_map/attend_and_decode/pallas_call | solution.py:423
  64.6 0.7 %copy.14 = bf16[2,4,32,192]{3,2,1,0:T(8,128)(2,1)} copy(bf16[2,4,32,192]{3,2,1,0:T(8,128)(2,1)S(1)} %bitcast.9) | data formatting | bytes 196608

commit v3 on v2

--- a/solution.py
+++ b/solution.py
@@ -36,7 +36,7 @@
     q_in, k_in, v_in, base_far, proj_far, std_far, mean_far, w_in_far, b_in_far, gain_far, w_up_far, b_up_far,
     out_ref,
     keys, values, v_row, queries, turned_queries, top, fade, weighted, summed, turned, sending, parts, lat_own, lat_near,
-    base_ref, proj_ref, std_ref, mean_ref, w_in, b_in_ref, gain_ref, w_up, b_up_ref, w_two, enlarged, columns, spread, pick, affine,
+    base_ref, proj_ref, std_ref, mean_ref, w_in, b_in_ref, gain_ref, w_up, b_up_ref, w_two, enlarged, shifted, spread, pick, affine,
     plane_send, plane_recv, ring_send, ring_recv, part_send, part_recv, near_send, near_recv, weight_sem,
 ):
     s, g = lax.axis_index("seq"), lax.axis_index("head")
@@ -141,19 +141,6 @@
     ]
     for copy in parameters:
         copy.start()
-
-    for copy in parameters:
-        copy.wait()
-    w_two[...] = jnp.zeros_like(w_two)
-    for t in range(3):
-        for u in range(3):
-            piece = w_in[(t * 3 + u) * 48 : (t * 3 + u) * 48 + 48, :]
-            for half in range(2):
-                at = t * 256 + (u + half) * 64
-                w_two[at : at + 48, half * CH : half * CH + CH] = piece
-
-    enlarged[...] = jnp.zeros_like(enlarged)
-    turned[...] = jnp.zeros_like(turned)
 
     def joined(pieces, axis):
         return pieces[0] if len(pieces) == 1 else jnp.concatenate(pieces, axis=axis)
@@ -200,6 +187,19 @@
     pass_on(0, 1, 0)
     pass_on(0, 1, 1)
     pass_on(1, 1, 0)
+
+    for copy in parameters:
+        copy.wait()
+    w_two[...] = jnp.zeros_like(w_two)
+    for t in range(3):
+        for u in range(3):
+            piece = w_in[(t * 3 + u) * 48 : (t * 3 + u) * 48 + 48, :]
+            for half in range(2):
+                at = t * 256 + (u + half) * 64
+                w_two[at : at + 48, half * CH : half * CH + CH] = piece
+
+    enlarged[...] = jnp.zeros_like(enlarged)
+    turned[...] = jnp.zeros_like(turned)
 
     def ones_where(shape, made):
         r = lax.broadcasted_iota(jnp.int32, shape, 0)
@@ -373,21 +373,17 @@
                             ]
 
     for v in range(3):
-        for f in range(2):
-            for y in range(4):
-                piece = [enlarged[tile, f * 4 + y, EDGE - 1 + v : EDGE + 31 + v, :] for tile in range(3)]
-                piece = jnp.concatenate(piece, axis=1).astype(BF16)
-                for line_out in range(4):
-                    for u in range(3):
-                        if (line_out + u + 1) // 2 == y:
-                            at = (f * 4 + line_out) * 32
-                            to = (u * 3 + v) * CH
-                            columns[at : at + 32, to : to + CH] = piece
+        for line in range(8):
+            piece = [enlarged[tile, line, EDGE - 1 + v : EDGE + 31 + v, :] for tile in range(3)]
+            shifted[v, line] = jnp.concatenate(piece, axis=1).astype(BF16)
     planes = b_up_ref[...]
-    for tap in range(9):
-        planes = planes + dot(
-            columns[:, tap * CH : tap * CH + CH], w_up[tap * OUTCH : tap * OUTCH + OUTCH, :], ((1,), (1,))
-        )
+    for u in range(3):
+        for v in range(3):
+            tap = u * 3 + v
+            lines = [shifted[v, f * 4 + (line_out + u + 1) // 2] for f in range(2) for line_out in range(4)]
+            planes = planes + dot(
+                jnp.concatenate(lines, axis=0), w_up[tap * OUTCH : tap * OUTCH + OUTCH, :], ((1,), (1,))
+            )
     out_ref[...] = planes.astype(BF16)
 
     for kind in range(3):
@@ -451,7 +447,7 @@
             pltpu.VMEM((1, OUTCH), F32),
             pltpu.VMEM((768, 2 * CH), BF16),
             pltpu.VMEM((3, 8, LINE, 128), F32),
-            pltpu.VMEM((256, 9 * CH), BF16),
+            pltpu.VMEM((3, 8, 32, CH), BF16),
             pltpu.VMEM((MSG, NUM), BF16),
             pltpu.VMEM((2, 128, 128), BF16),
             pltpu.VMEM((8, 128), F32),

time: 65.4 us -> 65 us (level)
  no operation moved by 1% of the time
where the time goes in v3:
time: 65 us; the launch traced here: 64.9 us
  Pallas kernels  64.3 us (99%)
  local copies, waits for them, and re-layouts  0.66 us (1%)
    pallas_call x1, Pallas kernels, on_device(): pl.pallas_call(kernel, out_shape=pltpu.VMEM((256, OUTCH), BF16), in_specs...  64.3 us

profile of v3, /device:TPU:1, one launch (start us, length us, event | category | flops | bytes accessed | tf_op | source)
XLA Modules:
  0.0 64.9 jit_solution(4494241323821942713)
XLA Ops:
  0.0 64.3 %attend_and_decode.1 = bf16[256,192]{1,0:T(8,128)(2,1)S(1)} custom-call(bf16[16,3072]{1,0:T(8,128)(2,1)} %q_in.1, bf16[16,3072]{1,0:T(8,128)(2,1)} %k_in.1, bf16[16,3072]{1,0:T(8,128)(2,1)} %v_in.1, bf16[16,64]{1,0:T(8,128)(2,1)} %base_far.1, bf16[64,384]{1,0:T(8,128)(2,1)} %bitcast.12, f32[1,16]{1,0:T(1,128)} %bitcast.14, f32[1,16]{1,0:T(1,128)} %bitcast.15, ...), custom_call_target="tpu_custom_call" | custom-call | tf_op jit(solution)/shard_map/attend_and_decode/pallas_call | solution.py:419
  64.3 0.7 %copy.14 = bf16[2,4,32,192]{3,2,1,0:T(8,128)(2,1)} copy(bf16[2,4,32,192]{3,2,1,0:T(8,128)(2,1)S(1)} %bitcast.9) | data formatting | bytes 196608

commit v4 on v3

--- a/solution.py
+++ b/solution.py
@@ -58,10 +58,10 @@
 
     barrier = pltpu.get_barrier_semaphore()
 
+    for other in (up, down, (after, g), (before, g), (after, last_g), (before, last_g)):
+        pl.semaphore_signal(barrier, inc=1, device_id=other, device_id_type=MESH)
     for i in range(1, PLACES):
         pl.semaphore_signal(barrier, inc=1, device_id=peer(i)[1], device_id_type=MESH)
-    for other in (up, down, (after, g), (before, g), (after, last_g), (before, last_g)):
-        pl.semaphore_signal(barrier, inc=1, device_id=other, device_id_type=MESH)
 
     q_row = queries.at[pl.ds(pl.multiple_of(row * ROW, ROW), ROW)]
     rows_of = ((k_in, keys.at[0]), (v_in, v_row), (q_in, q_row))

time: 65 us -> 65.1 us (level)
  no operation moved by 1% of the time
where the time goes in v4:
time: 65.1 us; the launch traced here: 65 us
  Pallas kernels  64.3 us (99%)
  local copies, waits for them, and re-layouts  0.66 us (1%)
    pallas_call x1, Pallas kernels, on_device(): pl.pallas_call(kernel, out_shape=pltpu.VMEM((256, OUTCH), BF16), in_specs...  64.3 us

profile of v4, /device:TPU:1, one launch (start us, length us, event | category | flops | bytes accessed | tf_op | source)
XLA Modules:
  0.0 65.0 jit_solution(15334101937689372478)
XLA Ops:
  0.0 64.3 %attend_and_decode.1 = bf16[256,192]{1,0:T(8,128)(2,1)S(1)} custom-call(bf16[16,3072]{1,0:T(8,128)(2,1)} %q_in.1, bf16[16,3072]{1,0:T(8,128)(2,1)} %k_in.1, bf16[16,3072]{1,0:T(8,128)(2,1)} %v_in.1, bf16[16,64]{1,0:T(8,128)(2,1)} %base_far.1, bf16[64,384]{1,0:T(8,128)(2,1)} %bitcast.12, f32[1,16]{1,0:T(1,128)} %bitcast.14, f32[1,16]{1,0:T(1,128)} %bitcast.15, ...), custom_call_target="tpu_custom_call" | custom-call | tf_op jit(solution)/shard_map/attend_and_decode/pallas_call | solution.py:419
  64.3 0.7 %copy.14 = bf16[2,4,32,192]{3,2,1,0:T(8,128)(2,1)} copy(bf16[2,4,32,192]{3,2,1,0:T(8,128)(2,1)S(1)} %bitcast.9) | data formatting | bytes 196608
